TPU v7x, 256 devices: a whole 4x4x8 slice. The times are simulated.
256 devices in a mesh: cols: 16 (over z_lo, y, core), cells: 16 (over x, z_hi).
Axes of the slice: x: 4, y: 4, z: 8 (z_hi: 4, z_lo: 2; z = z_hi * 2 + z_lo), core: 2. Of those that a mesh axis runs over, the one named last changes fastest.
Arguments:
- slab_cols: float32 [1024, 131072], P('cols', 'cells'), may hold values from -6 to 6
- observed_cov: float32 [2, 16, 131072], P(None, 'cols', 'cells'), may hold values from -1 to 30, as said below
- observed_cells: int32 [2, 16], replicated, may hold values from 0 to 131071, as said below
- noise_variance: float32 [2, 16], replicated, may hold values from 1 to 8
- wind_across: float32 [256, 512], P('cells'), may hold values from 0.25 to 0.5
- wind_along: float32 [256, 512], P('cells'), may hold values from -0.3 to 0.3
- diffusion: float32 [256, 512], P('cells'), may hold values from 0.125 to 0.25
Outputs:
- forecast: float32 [1024, 131072], P('cols', 'cells')
Inputs may be any that keep to these rules, and one draw needn't show every extreme that they name: `observed_cells`: the 32 observed cells are all different, so the two updates observe different cells. observed_cov[u, k, observed_cells[u, k]] lies between 20 and 30; every other entry lies between -1 and 1.
All inputs are finite; a program needn't handle non-finite values.
Results may differ from a plain program's by a relative error of at most 0.00012.
Values sent between devices are 32-bit elements; how exact they have to be, the bound alone decides.
A program may use at most 64 MiB of HBM per device.

v0:
```python
import jax
import jax.numpy as jnp
from jax import lax
from jax.experimental import pallas as pl
from jax.experimental.pallas import tpu as pltpu
from jax.sharding import PartitionSpec as P

SECTIONS = 8
GROUP = 8
LANES = 128
AHEAD = 3
MESH = pl.DeviceIdType.MESH


def place(k):
    return (k % 2) * 8 + ((k // 2) % 4) * 2 + k // 8


def kernel(
    cells_ref, noise_ref, slab_ref, cov_ref, across_ref, along_ref, spread_ref, out_ref,
    own, low, high, flat, head, natural, coef, buf_a, buf_b, gathered, corr, result, weight,
    msg_x, slots_x, msg_z, slots_z, msg_c, slots_c,
    local_sem, out_sem, halo_send, halo_recv, head_send, head_recv,
    x_send, x_recv, z_send, z_recv, c_send, c_recv,
    pair_send, pair_recv, y_send, y_recv, core_send, core_recv,
):
    columns, local_cells = slab_ref.shape
    grid_rows, width = across_ref.shape
    count = cells_ref.shape[1]
    total = 2 * count
    groups = columns // GROUP
    edge = SECTIONS * width
    extent = grid_rows + 2 * SECTIONS

    c = lax.axis_index("cols")
    t = lax.axis_index("cells")
    core, y, z_lo = lax.rem(c, 2), lax.rem(lax.div(c, 2), 4), lax.div(c, 8)
    x, z_hi = lax.div(t, 4), lax.rem(t, 4)
    mine = core * 8 + y * 2 + z_lo
    after, before = lax.rem(t + 1, 16), lax.rem(t + 15, 16)

    def cells_device(target):
        return {"cells": target}

    def cols_device(target):
        return {"cols": target}

    def remote(src, dst, send, recv, device):
        return pltpu.make_async_remote_copy(
            src_ref=src, dst_ref=dst, send_sem=send, recv_sem=recv, device_id=device, device_id_type=MESH
        )

    x_peers = [lax.rem(x + d, 4) for d in range(1, 4)]
    z_peers = [lax.rem(z_hi + d, 4) for d in range(1, 4)]
    c_peers = [lax.rem(c + d, 16) for d in range(1, 16)]
    y_peers = [lax.rem(y + d, 4) for d in range(1, 4)]

    locals_ = [
        pltpu.make_async_copy(cov_ref, flat, local_sem.at[0]),
        pltpu.make_async_copy(across_ref, head.at[0, SECTIONS : SECTIONS + grid_rows], local_sem.at[1]),
        pltpu.make_async_copy(along_ref, head.at[1, SECTIONS : SECTIONS + grid_rows], local_sem.at[2]),
        pltpu.make_async_copy(spread_ref, head.at[2, SECTIONS : SECTIONS + grid_rows], local_sem.at[3]),
        pltpu.make_async_copy(slab_ref, own, local_sem.at[4]),
    ]
    for copy in locals_:
        copy.start()

    barrier = pltpu.get_barrier_semaphore()
    peers = (
        [cells_device(after), cells_device(before)]
        + [cells_device(p * 4 + z_hi) for p in x_peers]
        + [cells_device(x * 4 + p) for p in z_peers]
        + [cols_device(p) for p in c_peers]
    )
    for device in peers:
        pl.semaphore_signal(barrier, inc=1, device_id=device, device_id_type=MESH)

    for copy in locals_[:4]:
        copy.wait()
    for u in range(2):
        for i in range(grid_rows):
            head[3 + u, SECTIONS + i : SECTIONS + i + 1, :] = flat[u, :, i * width : (i + 1) * width]
    pl.semaphore_wait(barrier, len(peers))

    top = SECTIONS + grid_rows
    head_up = remote(
        head.at[:, grid_rows : grid_rows + SECTIONS, :], head.at[:, 0:SECTIONS, :],
        head_send.at[0], head_recv.at[0], cells_device(after),
    )
    head_down = remote(
        head.at[:, SECTIONS : 2 * SECTIONS, :], head.at[:, top : top + SECTIONS, :],
        head_send.at[1], head_recv.at[1], cells_device(before),
    )
    head_up.start()
    head_down.start()

    def halos(g):
        rows = pl.ds(pl.multiple_of(g * GROUP, GROUP), GROUP)
        return (
            remote(
                slab_ref.at[rows, local_cells - edge : local_cells], low.at[rows, :],
                halo_send.at[0, g], halo_recv.at[0, g], cells_device(after),
            ),
            remote(
                slab_ref.at[rows, 0:edge], high.at[rows, :],
                halo_send.at[1, g], halo_recv.at[1, g], cells_device(before),
            ),
        )

    for g in range(AHEAD):
        for copy in halos(g):
            copy.start()

    locals_[4].wait()
    part = 2 * width
    row_q = lax.broadcasted_iota(jnp.int32, (total, LANES), 0)
    wanted = jnp.zeros((total, LANES), jnp.int32)
    for u in range(2):
        for k in range(count):
            wanted = jnp.where(row_q == place(k) * 2 + u, cells_ref[u, k], wanted)
    wanted = jnp.concatenate([wanted] * (part // LANES), axis=1) - t * local_cells
    lane = lax.broadcasted_iota(jnp.int32, (total, part), 1)
    sub_8 = lax.broadcasted_iota(jnp.int32, (GROUP, part), 0)
    first_row = 2 * lax.rem(mine, 4)
    bf16 = jnp.bfloat16

    def pick(n, found):
        start = pl.multiple_of(n * part, part)
        chosen = jnp.where(lane + start == wanted, 1.0, 0.0).astype(bf16)
        rows = jnp.where(
            sub_8 == first_row,
            flat[0, :, pl.ds(start, part)],
            jnp.where(sub_8 == first_row + 1, flat[1, :, pl.ds(start, part)], 0.0),
        )
        block = jnp.concatenate([own[:, pl.ds(start, part)], rows, jnp.zeros_like(rows)], axis=0)
        upper = block.astype(bf16)
        rest = block - upper.astype(jnp.float32)
        middle = rest.astype(bf16)
        lower = (rest - middle.astype(jnp.float32)).astype(bf16)
        pieces = jnp.concatenate([upper, middle, lower], axis=0)
        return found + lax.dot_general(
            pieces, chosen, (((1,), (1,)), ((), ())), preferred_element_type=jnp.float32
        )

    height = columns + 2 * GROUP
    found = lax.fori_loop(
        0, local_cells // part, pick, jnp.zeros((3 * height, total), jnp.float32)
    )
    found = found[0:height] + found[height : 2 * height] + found[2 * height : 3 * height]
    found = jnp.concatenate([found, jnp.zeros((height, LANES - total), jnp.float32)], axis=1)
    square = jnp.concatenate(
        [
            jnp.zeros((total, LANES), jnp.float32),
            found[0:columns],
            jnp.zeros((LANES - total - columns, LANES), jnp.float32),
        ],
        axis=0,
    )
    tile = found[columns : columns + GROUP]
    msg_x[0:total, :] = square.T[0:total, :]
    msg_x[total : total + GROUP, :] = tile

    x_copies = [
        remote(msg_x, slots_x.at[x], x_send.at[p], x_recv.at[x], cells_device(p * 4 + z_hi)) for p in x_peers
    ]
    for copy in x_copies:
        copy.start()

    head_up.wait_recv()
    head_down.wait_recv()
    half_across = 0.5 * head[0]
    half_along = 0.5 * head[1]
    spread = head[2]
    values = [
        1.0 - 4.0 * spread, spread - half_across, spread + half_across, spread - half_along, spread + half_along
    ]
    for n in range(5):
        natural[n] = values[n]

    def widen(r, carry):
        for n in range(5):
            coef[n, r] = jnp.broadcast_to(natural[n, pl.ds(r, 1), :], (GROUP, width))
        return carry

    lax.fori_loop(1, extent - 1, widen, 0)

    def cov_section(_, fields):
        new = []
        for f in fields:
            new.append(
                values[0] * f
                + values[1] * pltpu.roll(f, extent - 1, 0)
                + values[2] * pltpu.roll(f, 1, 0)
                + values[3] * pltpu.roll(f, width - 1, 1)
                + values[4] * pltpu.roll(f, 1, 1)
            )
        return tuple(new)

    fields = lax.fori_loop(0, SECTIONS, cov_section, (head[3], head[4]))
    span = 2 * grid_rows

    def block_of(position, blocks=1):
        return gathered.at[:, pl.ds(pl.multiple_of(position * span, span), blocks * span), :]

    for u in range(2):
        rows = pl.ds(pl.multiple_of(mine * span + u * grid_rows, grid_rows), grid_rows)
        for v in range(width // LANES):
            gathered[v, rows, :] = fields[u][SECTIONS:top, v * LANES : (v + 1) * LANES]
    pair = core * 8 + y * 2 + (1 - z_lo)
    pair_copy = remote(
        block_of(mine), block_of(mine), pair_send, pair_recv, cols_device((1 - z_lo) * 8 + y * 2 + core)
    )
    pair_copy.start()

    for p, copy in zip(x_peers, x_copies):
        remote(msg_x, slots_x.at[p], x_send.at[p], x_recv.at[p], cells_device(p * 4 + z_hi)).wait_recv()
    summed = msg_x[...]
    for p in x_peers:
        summed = summed + slots_x[p]
    msg_z[...] = summed
    z_copies = [
        remote(msg_z, slots_z.at[z_hi], z_send.at[p], z_recv.at[z_hi], cells_device(x * 4 + p)) for p in z_peers
    ]
    for copy in z_copies:
        copy.start()

    def stencil(g):
        rows = pl.ds(pl.multiple_of(g * GROUP, GROUP), GROUP)

        def read(r, section):
            if section == 0:
                if r < SECTIONS:
                    return low[rows, r * width : (r + 1) * width]
                if r < top:
                    return own[rows, (r - SECTIONS) * width : (r - SECTIONS + 1) * width]
                return high[rows, (r - top) * width : (r - top + 1) * width]
            return (buf_a if section % 2 else buf_b)[r]

        for section in range(SECTIONS):
            first, last = section + 1, extent - section - 1
            below, here = read(first - 1, section), read(first, section)
            for r in range(first, last):
                above = read(r + 1, section)
                new = (
                    coef[0, r] * here
                    + coef[1, r] * above
                    + coef[2, r] * below
                    + coef[3, r] * pltpu.roll(here, width - 1, 1)
                    + coef[4, r] * pltpu.roll(here, 1, 1)
                )
                if section == SECTIONS - 1:
                    result[rows, (r - SECTIONS) * width : (r - SECTIONS + 1) * width] = new
                else:
                    (buf_b if section % 2 else buf_a)[r] = new
                below, here = here, above

    def finish(g):
        rows = pl.ds(pl.multiple_of(g * GROUP, GROUP), GROUP)
        for i in range(grid_rows):
            part = slice(i * width, (i + 1) * width)
            result[rows, part] = result[rows, part] - corr[i, rows, :]
        pltpu.make_async_copy(result.at[rows, :], out_ref.at[rows, :], out_sem.at[g]).start()

    def after_first():
        remote(block_of(pair), block_of(pair), pair_send, pair_recv, cols_device((1 - z_lo) * 8 + y * 2 + core)).wait_recv()
        here = block_of(core * 8 + y * 2, 2)
        for p in y_peers:
            remote(here, here, y_send.at[p], y_recv.at[y], cols_device(z_lo * 8 + p * 2 + core)).start()
        for p in z_peers:
            remote(msg_z, slots_z.at[p], z_send.at[p], z_recv.at[p], cells_device(x * 4 + p)).wait_recv()
        summed = msg_z[...]
        for p in z_peers:
            summed = summed + slots_z[p]
        msg_c[...] = summed
        for p in c_peers:
            remote(
                msg_c.at[total : total + GROUP, :], slots_c.at[c], c_send.at[p], c_recv.at[c], cols_device(p)
            ).start()
        slots_c[c] = summed[total : total + GROUP, :]

    def after_second():
        for p in y_peers:
            there = block_of(core * 8 + p * 2, 2)
            remote(there, there, y_send.at[p], y_recv.at[p], cols_device(z_lo * 8 + p * 2 + core)).wait_recv()
        half = block_of(core * 8, 8)
        remote(half, half, core_send, core_recv, cols_device(z_lo * 8 + y * 2 + (1 - core))).start()
        for p in c_peers:
            remote(
                msg_c.at[total : total + GROUP, :], slots_c.at[p], c_send.at[p], c_recv.at[p], cols_device(p)
            ).wait_recv()
        order = sorted(range(count), key=place)
        quarters = []
        for b in range(4):
            quarter = slots_c[order[4 * b]]
            for n in range(1, 4):
                quarter = quarter + slots_c[order[4 * b + n]]
            quarters.append(quarter)
        entries = jnp.concatenate(quarters, axis=0)
        turned = jnp.concatenate(
            [entries, jnp.zeros((LANES - total, LANES), jnp.float32)], axis=0
        ).T[0:total, :]
        row = lax.broadcasted_iota(jnp.int32, (total, LANES), 0)
        col = lax.broadcasted_iota(jnp.int32, (total, LANES), 1)
        row_u, col_u = jnp.bitwise_and(row, 1), jnp.bitwise_and(col, 1)
        system = jnp.where(
            row_u == col_u, 0.5 * (entries + turned), jnp.where(row_u < col_u, entries, turned)
        )
        noise = jnp.zeros((total, LANES), jnp.float32)
        for u in range(2):
            for k in range(count):
                noise = jnp.where(row == place(k) * 2 + u, noise_ref[u, k], noise)
        system = system + jnp.where(row == col, noise, 0.0)
        system = jnp.where(col < total, system, msg_c[0:total, :])
        for u in range(2):
            for k in range(count):
                q = place(k) * 2 + u
                scaled = system[q : q + 1, :] / system[q : q + 1, q : q + 1]
                system = jnp.where(row == q, scaled, system - system[:, q : q + 1] * scaled)
        weights = jnp.concatenate(
            [system, jnp.zeros((LANES - total, LANES), jnp.float32)], axis=0
        ).T[total : total + columns, :]
        upper = weights.astype(jnp.bfloat16).astype(jnp.float32)
        lower = weights - upper
        weight[...] = (
            upper + pltpu.roll(upper, total, 1) + pltpu.roll(lower, 2 * total, 1) + pltpu.roll(lower, 3 * total, 1)
        )

    def after_third():
        there = block_of((1 - core) * 8, 8)
        remote(there, there, core_send, core_recv, cols_device(z_lo * 8 + y * 2 + (1 - core))).wait_recv()
        left = weight[...].astype(jnp.bfloat16)

        def one_row(i, carry):
            rows = jnp.concatenate(
                [gathered[v, pl.ds(i, total, stride=grid_rows), :] for v in range(width // LANES)], axis=1
            )
            upper = rows.astype(jnp.bfloat16)
            lower = (rows - upper.astype(jnp.float32)).astype(jnp.bfloat16)
            right = jnp.concatenate([upper, lower, upper, lower], axis=0)
            corr[i] = jnp.dot(left, right, preferred_element_type=jnp.float32)
            return carry

        lax.fori_loop(0, grid_rows, one_row, 0)

    def step(g, carry):
        for copy in halos(g):
            copy.wait_recv()

        stencil(g)

        @pl.when(g == 0)
        def _():
            after_first()

        @pl.when(g == 1)
        def _():
            after_second()

        @pl.when(g == 2)
        def _():
            after_third()
            finish(0)
            finish(1)

        @pl.when(g >= 2)
        def _():
            finish(g)

        for copy in halos(g):
            copy.wait_send()

        @pl.when(g + AHEAD < groups)
        def _():
            for copy in halos(g + AHEAD):
                copy.start()

        return carry

    lax.fori_loop(0, groups, step, 0)

    for copy in [head_up, head_down, pair_copy]:
        copy.wait_send()
    for copy in x_copies + z_copies:
        copy.wait_send()
    for p in y_peers:
        here = block_of(core * 8 + y * 2, 2)
        remote(here, here, y_send.at[p], y_recv.at[p], cols_device(z_lo * 8 + p * 2 + core)).wait_send()
    half = block_of(core * 8, 8)
    remote(half, half, core_send, core_recv, cols_device(z_lo * 8 + y * 2 + (1 - core))).wait_send()
    for p in c_peers:
        remote(
            msg_c.at[total : total + GROUP, :], slots_c.at[c], c_send.at[p], c_recv.at[p], cols_device(p)
        ).wait_send()
    for g in range(groups):
        rows = pl.ds(g * GROUP, GROUP)
        pltpu.make_async_copy(result.at[rows, :], out_ref.at[rows, :], out_sem.at[g]).wait()


def local(
    slab_cols, observed_cov, observed_cells, noise_variance, wind_across, wind_along, diffusion
):
    columns, local_cells = slab_cols.shape
    grid_rows, width = wind_across.shape
    count = observed_cells.shape[1]
    total = 2 * count
    extent = grid_rows + 2 * SECTIONS
    edge = SECTIONS * width
    groups = columns // GROUP
    f32 = jnp.float32
    dma = pltpu.SemaphoreType.DMA
    any_space = pl.BlockSpec(memory_space=pltpu.HBM)
    scalars = pl.BlockSpec(memory_space=pltpu.SMEM)
    return pl.pallas_call(
        kernel,
        out_shape=jax.ShapeDtypeStruct((columns, local_cells), f32),
        in_specs=[scalars, scalars] + [any_space] * 5,
        out_specs=pl.BlockSpec(memory_space=pl.ANY),
        scratch_shapes=[
            pltpu.VMEM((columns, local_cells), f32),
            pltpu.VMEM((columns, edge), f32),
            pltpu.VMEM((columns, edge), f32),
            pltpu.VMEM((2, 1, local_cells), f32),
            pltpu.VMEM((5, extent, width), f32),
            pltpu.VMEM((5, extent, width), f32),
            pltpu.VMEM((5, extent, GROUP, width), f32),
            pltpu.VMEM((extent, GROUP, width), f32),
            pltpu.VMEM((extent, GROUP, width), f32),
            pltpu.VMEM((width // LANES, total * grid_rows, LANES), f32),
            pltpu.VMEM((grid_rows, columns, width), f32),
            pltpu.VMEM((columns, local_cells), f32),
            pltpu.VMEM((columns, LANES), f32),
            pltpu.VMEM((total + GROUP, LANES), f32),
            pltpu.VMEM((4, total + GROUP, LANES), f32),
            pltpu.VMEM((total + GROUP, LANES), f32),
            pltpu.VMEM((4, total + GROUP, LANES), f32),
            pltpu.VMEM((total + GROUP, LANES), f32),
            pltpu.VMEM((16, GROUP, LANES), f32),
            dma((5,)),
            dma((groups,)),
            dma((2, groups)),
            dma((2, groups)),
            dma((2,)),
            dma((2,)),
            dma((4,)),
            dma((4,)),
            dma((4,)),
            dma((4,)),
            dma((16,)),
            dma((16,)),
            dma,
            dma,
            dma((4,)),
            dma((4,)),
            dma,
            dma,
        ],
        compiler_params=pltpu.CompilerParams(
            collective_id=0, has_side_effects=True, vmem_limit_bytes=60 * 1024 * 1024
        ),
    )(observed_cells, noise_variance, slab_cols, observed_cov, wind_across, wind_along, diffusion)


def solution(mesh):
    return jax.shard_map(
        local,
        mesh=mesh,
        in_specs=(
            P("cols", "cells"),
            P(None, "cols", "cells"),
            P(),
            P(),
            P("cells", None),
            P("cells", None),
            P("cells", None),
        ),
        out_specs=P("cols", "cells"),
        check_vma=False,
    )
```

profile of v0, /device:TPU:1, one launch (start us, length us, event | category | flops | bytes accessed | tf_op | source)
XLA Modules:
  0.0 78.5 jit_solution(11229623297323886928)
XLA Ops:
  0.0 75.5 %shard_map.73 = f32[64,8192]{1,0:T(8,128)} custom-call(s32[2,16]{1,0:T(2,128)} %cells_ref.1, f32[2,16]{1,0:T(2,128)} %noise_ref.1, f32[64,8192]{1,0:T(8,128)} %slab_ref.1, f32[2,1,8192]{2,1,0:T(1,128)} %cov_ref.1, f32[16,512]{1,0:T(8,128)} %across_ref.1, f32[16,512]{1,0:T(8,128)} %along_ref.1, f32[16,512]{1,0:T(8,128)} %spread_ref.1), custom_call_target="tpu_custom_call" | custom-call | tf_op jit(solution)/shard_map/pallas_call | solution.py:413
  75.5 3.1 %copy.9 = f32[64,8192]{1,0:T(8,128)} copy(f32[64,8192]{1,0:T(8,128)} %shard_map.73) | data formatting | bytes 4194304
where the time goes:
time: 78.7 us; the launch traced here: 78.5 us
  Pallas kernels  75.5 us (96%)
  local copies, waits for them, and re-layouts  3.06 us (4%)
    pallas_call x1, Pallas kernels, local(): pl.pallas_call(kernel, out_shape=jax.ShapeDtypeStruct((columns, local_cel...  75.5 us
    unnamed x1, local copies, waits for them, and re-layouts  3.06 us

commit v1 on v0

v1 whole, which is shorter than its diff:
```python
import jax
import jax.numpy as jnp
from jax import lax
from jax.experimental import pallas as pl
from jax.experimental.pallas import tpu as pltpu
from jax.sharding import PartitionSpec as P

SECTIONS = 8
GROUP = 8
LANES = 128
AHEAD = 6
STEP_X, STEP_PAIR, STEP_Y, STEP_CORE, STEP_CORR = 0, 3, 6, 9, 11
MESH = pl.DeviceIdType.MESH


def place(k):
    return (k % 2) * 8 + ((k // 2) % 4) * 2 + k // 8


def kernel(
    cells_ref, noise_ref, slab_ref, cov_ref, across_ref, along_ref, spread_ref, result,
    own, low, high, flat, head, natural, coef, buf_a, buf_b, gathered, corr, weight, right_side,
    msg_x, slots_x, msg_z, slots_z, msg_c, slots_c,
    local_sem, halo_send, halo_recv, head_send, head_recv,
    x_send, x_recv, z_send, z_recv, e_send, e_recv,
    pair_send, pair_recv, y_send, y_recv, core_send, core_recv,
):
    columns, local_cells = slab_ref.shape
    grid_rows, width = across_ref.shape
    count = cells_ref.shape[1]
    total = 2 * count
    groups = columns // GROUP
    edge = SECTIONS * width
    extent = grid_rows + 2 * SECTIONS

    c = lax.axis_index("cols")
    t = lax.axis_index("cells")
    core, y, z_lo = lax.rem(c, 2), lax.rem(lax.div(c, 2), 4), lax.div(c, 8)
    x, z_hi = lax.div(t, 4), lax.rem(t, 4)
    mine = core * 8 + y * 2 + z_lo
    after, before = lax.rem(t + 1, 16), lax.rem(t + 15, 16)

    def cells_device(target):
        return {"cells": target}

    def cols_device(target):
        return {"cols": target}

    def remote(src, dst, send, recv, device):
        return pltpu.make_async_remote_copy(
            src_ref=src, dst_ref=dst, send_sem=send, recv_sem=recv, device_id=device, device_id_type=MESH
        )

    x_peers = [lax.rem(x + d, 4) for d in range(1, 4)]
    z_peers = [lax.rem(z_hi + d, 4) for d in range(1, 4)]
    y_peers = [lax.rem(y + d, 4) for d in range(1, 4)]

    locals_ = [
        pltpu.make_async_copy(cov_ref, flat, local_sem.at[0]),
        pltpu.make_async_copy(across_ref, head.at[0, SECTIONS : SECTIONS + grid_rows], local_sem.at[1]),
        pltpu.make_async_copy(along_ref, head.at[1, SECTIONS : SECTIONS + grid_rows], local_sem.at[2]),
        pltpu.make_async_copy(spread_ref, head.at[2, SECTIONS : SECTIONS + grid_rows], local_sem.at[3]),
        pltpu.make_async_copy(slab_ref, own, local_sem.at[4]),
    ]
    for copy in locals_:
        copy.start()

    barrier = pltpu.get_barrier_semaphore()
    peers = (
        [cells_device(after), cells_device(before)]
        + [cells_device(p * 4 + z_hi) for p in x_peers]
        + [cells_device(x * 4 + p) for p in z_peers]
        + [cols_device(z_lo * 8 + p * 2 + core) for p in y_peers]
        + [cols_device(z_lo * 8 + p * 2 + (1 - core)) for p in y_peers]
        + [cols_device((1 - z_lo) * 8 + y * 2 + core), cols_device(z_lo * 8 + y * 2 + (1 - core))]
    )
    for device in peers:
        pl.semaphore_signal(barrier, inc=1, device_id=device, device_id_type=MESH)

    for copy in locals_[:4]:
        copy.wait()
    for u in range(2):
        for i in range(grid_rows):
            head[3 + u, SECTIONS + i : SECTIONS + i + 1, :] = flat[u, :, i * width : (i + 1) * width]
    locals_[4].wait()
    part = 2 * width
    row_q = lax.broadcasted_iota(jnp.int32, (total, LANES), 0)
    wanted = jnp.zeros((total, LANES), jnp.int32)
    for u in range(2):
        for k in range(count):
            wanted = jnp.where(row_q == place(k) * 2 + u, cells_ref[u, k], wanted)
    wanted = jnp.concatenate([wanted] * (part // LANES), axis=1) - t * local_cells
    lane = lax.broadcasted_iota(jnp.int32, (total, part), 1)
    sub_8 = lax.broadcasted_iota(jnp.int32, (GROUP, part), 0)
    first_row = 2 * lax.rem(mine, 4)
    bf16 = jnp.bfloat16

    def pick(n, found):
        start = pl.multiple_of(n * part, part)
        chosen = jnp.where(lane + start == wanted, 1.0, 0.0).astype(bf16)
        rows = jnp.where(
            sub_8 == first_row,
            flat[0, :, pl.ds(start, part)],
            jnp.where(sub_8 == first_row + 1, flat[1, :, pl.ds(start, part)], 0.0),
        )
        block = jnp.concatenate([own[:, pl.ds(start, part)], rows, jnp.zeros_like(rows)], axis=0)
        upper = block.astype(bf16)
        rest = block - upper.astype(jnp.float32)
        middle = rest.astype(bf16)
        lower = (rest - middle.astype(jnp.float32)).astype(bf16)
        pieces = jnp.concatenate([upper, middle, lower], axis=0)
        return found + lax.dot_general(
            pieces, chosen, (((1,), (1,)), ((), ())), preferred_element_type=jnp.float32
        )

    height = columns + 2 * GROUP
    found = lax.fori_loop(
        0, local_cells // part, pick, jnp.zeros((3 * height, total), jnp.float32)
    )
    found = found[0:height] + found[height : 2 * height] + found[2 * height : 3 * height]
    found = jnp.concatenate([found, jnp.zeros((height, LANES - total), jnp.float32)], axis=1)
    square = jnp.concatenate(
        [
            jnp.zeros((total, LANES), jnp.float32),
            found[0:columns],
            jnp.zeros((LANES - total - columns, LANES), jnp.float32),
        ],
        axis=0,
    )
    tile = found[columns : columns + GROUP]
    msg_z[0:total, :] = square.T[0:total, :]
    msg_z[total : total + GROUP, :] = tile

    pl.semaphore_wait(barrier, len(peers))

    top = SECTIONS + grid_rows
    head_up = remote(
        head.at[:, grid_rows : grid_rows + SECTIONS, :], head.at[:, 0:SECTIONS, :],
        head_send.at[0], head_recv.at[0], cells_device(after),
    )
    head_down = remote(
        head.at[:, SECTIONS : 2 * SECTIONS, :], head.at[:, top : top + SECTIONS, :],
        head_send.at[1], head_recv.at[1], cells_device(before),
    )
    z_copies = [
        remote(msg_z, slots_z.at[z_hi], z_send.at[p], z_recv.at[z_hi], cells_device(x * 4 + p)) for p in z_peers
    ]
    for copy in z_copies:
        copy.start()
    head_up.start()
    head_down.start()

    def halos(n):
        rows = pl.ds(pl.multiple_of(lax.div(n, 2) * GROUP, GROUP), GROUP)
        piece = edge // 2
        shift = lax.rem(n, 2) * piece
        here = pl.ds(pl.multiple_of(shift, piece), piece)
        last = pl.ds(pl.multiple_of(local_cells - edge + shift, piece), piece)
        return (
            remote(
                slab_ref.at[rows, last], low.at[rows, here],
                halo_send.at[0, n], halo_recv.at[0, n], cells_device(after),
            ),
            remote(
                slab_ref.at[rows, here], high.at[rows, here],
                halo_send.at[1, n], halo_recv.at[1, n], cells_device(before),
            ),
        )

    for n in range(AHEAD):
        for copy in halos(n):
            copy.start()

    other = core * 8 + y * 2 + (1 - z_lo)
    span = 2 * grid_rows

    def block_of(position, blocks=1):
        return gathered.at[:, pl.ds(pl.multiple_of(position * span, span), blocks * span), :]

    def x_copy(slot, p):
        return remote(msg_x, slots_x.at[slot], x_send.at[p], x_recv.at[slot], cells_device(p * 4 + z_hi))

    def pair_copy(position):
        return remote(
            block_of(position), block_of(position), pair_send.at[0], pair_recv.at[0],
            cols_device((1 - z_lo) * 8 + y * 2 + core),
        )

    def pair_entries(slot):
        return remote(
            msg_c, slots_c.at[slot], pair_send.at[1], pair_recv.at[1],
            cols_device((1 - z_lo) * 8 + y * 2 + core),
        )

    def y_copy(source, p):
        both = block_of(core * 8 + source * 2, 2)
        return remote(both, both, y_send.at[p], y_recv.at[source], cols_device(z_lo * 8 + p * 2 + core))

    def core_copy(source):
        half = block_of(source * 8, 8)
        return remote(half, half, core_send, core_recv, cols_device(z_lo * 8 + y * 2 + (1 - core)))

    others = [(core, p) for p in y_peers] + [(1 - core, p) for p in y_peers] + [(1 - core, y)]

    def entries_copy(source, target):
        mate = source[0] * 4 + source[1]
        two = slots_c.at[pl.ds(mate * 2, 2)]
        return remote(
            two, two, e_send.at[target[0] * 4 + target[1]], e_recv.at[mate],
            cols_device(z_lo * 8 + target[1] * 2 + target[0]),
        )

    def stencil(g):
        rows = pl.ds(pl.multiple_of(g * GROUP, GROUP), GROUP)

        def read(r, section):
            if section == 0:
                if r < SECTIONS:
                    return low[rows, r * width : (r + 1) * width]
                if r < top:
                    return own[rows, (r - SECTIONS) * width : (r - SECTIONS + 1) * width]
                return high[rows, (r - top) * width : (r - top + 1) * width]
            return (buf_a if section % 2 else buf_b)[r]

        for section in range(SECTIONS):
            first, last = section + 1, extent - section - 1
            below, here = read(first - 1, section), read(first, section)
            for r in range(first, last):
                above = read(r + 1, section)
                new = (
                    coef[0, r] * here
                    + coef[1, r] * above
                    + coef[2, r] * below
                    + coef[3, r] * pltpu.roll(here, width - 1, 1)
                    + coef[4, r] * pltpu.roll(here, 1, 1)
                )
                if section == SECTIONS - 1:
                    result[rows, (r - SECTIONS) * width : (r - SECTIONS + 1) * width] = new
                else:
                    (buf_b if section % 2 else buf_a)[r] = new
                below, here = here, above

    def finish(g):
        rows = pl.ds(pl.multiple_of(g * GROUP, GROUP), GROUP)
        for i in range(grid_rows):
            part = slice(i * width, (i + 1) * width)
            result[rows, part] = result[rows, part] - corr[i, rows, :]

    def send_x():
        for p in z_peers:
            remote(msg_z, slots_z.at[p], z_send.at[p], z_recv.at[p], cells_device(x * 4 + p)).wait_recv()
        summed = msg_z[...]
        for p in z_peers:
            summed = summed + slots_z[p]
        msg_x[...] = summed
        for p in x_peers:
            x_copy(x, p).start()

    def forecast_cov():
        head_up.wait_recv()
        head_down.wait_recv()
        half_across = 0.5 * head[0]
        half_along = 0.5 * head[1]
        spread = head[2]
        values = [
            1.0 - 4.0 * spread, spread - half_across, spread + half_across, spread - half_along, spread + half_along
        ]
        for n in range(5):
            natural[n] = values[n]

        def widen(r, carry):
            for n in range(5):
                coef[n, r] = jnp.broadcast_to(natural[n, pl.ds(r, 1), :], (GROUP, width))
            return carry

        lax.fori_loop(1, extent - 1, widen, 0)

        def cov_section(_, fields):
            new = []
            for f in fields:
                new.append(
                    values[0] * f
                    + values[1] * pltpu.roll(f, extent - 1, 0)
                    + values[2] * pltpu.roll(f, 1, 0)
                    + values[3] * pltpu.roll(f, width - 1, 1)
                    + values[4] * pltpu.roll(f, 1, 1)
                )
            return tuple(new)

        fields = lax.fori_loop(0, SECTIONS, cov_section, (head[3], head[4]))
        for u in range(2):
            rows = pl.ds(pl.multiple_of(mine * span + u * grid_rows, grid_rows), grid_rows)
            for v in range(width // LANES):
                gathered[v, rows, :] = fields[u][SECTIONS:top, v * LANES : (v + 1) * LANES]
        pair_copy(mine).start()

    def send_pair():
        for p in x_peers:
            x_copy(p, p).wait_recv()
        summed = msg_x[...]
        for p in x_peers:
            summed = summed + slots_x[p]
        right_side[...] = summed[0:total, :]
        msg_c[...] = summed[total : total + GROUP, :]
        slots_c[mine] = summed[total : total + GROUP, :]
        pair_entries(mine).start()
        pair_copy(other).wait_recv()
        for p in y_peers:
            y_copy(y, p).start()

    def send_entries():
        pair_entries(other).wait_recv()
        for target in others:
            entries_copy((core, y), target).start()

    def send_core():
        for p in y_peers:
            y_copy(p, p).wait_recv()
        core_copy(core).start()

    def solve():
        for source in others:
            entries_copy(source, source).wait_recv()
        quarters = []
        for b in range(4):
            quarter = slots_c[4 * b]
            for n in range(1, 4):
                quarter = quarter + slots_c[4 * b + n]
            quarters.append(quarter)
        entries = jnp.concatenate(quarters, axis=0)
        turned = jnp.concatenate(
            [entries, jnp.zeros((LANES - total, LANES), jnp.float32)], axis=0
        ).T[0:total, :]
        row = lax.broadcasted_iota(jnp.int32, (total, LANES), 0)
        col = lax.broadcasted_iota(jnp.int32, (total, LANES), 1)
        row_u, col_u = jnp.bitwise_and(row, 1), jnp.bitwise_and(col, 1)
        system = jnp.where(
            row_u == col_u, 0.5 * (entries + turned), jnp.where(row_u < col_u, entries, turned)
        )
        noise = jnp.zeros((total, LANES), jnp.float32)
        for u in range(2):
            for k in range(count):
                noise = jnp.where(row == place(k) * 2 + u, noise_ref[u, k], noise)
        system = system + jnp.where(row == col, noise, 0.0)
        system = jnp.where(col < total, system, right_side[...])
        for u in range(2):
            for k in range(count):
                q = place(k) * 2 + u
                scaled = system[q : q + 1, :] / system[q : q + 1, q : q + 1]
                system = jnp.where(row == q, scaled, system - system[:, q : q + 1] * scaled)
        weights = jnp.concatenate(
            [system, jnp.zeros((LANES - total, LANES), jnp.float32)], axis=0
        ).T[total : total + columns, :]
        upper = weights.astype(jnp.bfloat16).astype(jnp.float32)
        lower = weights - upper
        weight[...] = (
            upper + pltpu.roll(upper, total, 1) + pltpu.roll(lower, 2 * total, 1) + pltpu.roll(lower, 3 * total, 1)
        )

    def correct():
        core_copy(1 - core).wait_recv()
        left = weight[...].astype(jnp.bfloat16)

        def one_row(i, carry):
            rows = jnp.concatenate(
                [gathered[v, pl.ds(i, total, stride=grid_rows), :] for v in range(width // LANES)], axis=1
            )
            upper = rows.astype(jnp.bfloat16)
            lower = (rows - upper.astype(jnp.float32)).astype(jnp.bfloat16)
            right = jnp.concatenate([upper, lower, upper, lower], axis=0)
            corr[i] = jnp.dot(left, right, preferred_element_type=jnp.float32)
            return carry

        lax.fori_loop(0, grid_rows, one_row, 0)

    def advance(g):
        for h in range(2):
            for copy in halos(2 * g + h):
                copy.wait_recv()
        stencil(g)

    steps = 2 * groups

    def step(n, carry):
        @pl.when(n < steps)
        def _():
            for copy in halos(n):
                copy.wait_send()

        @pl.when(n + AHEAD < steps)
        def _():
            for copy in halos(n + AHEAD):
                copy.start()

        @pl.when(n == STEP_X)
        def _():
            send_x()
            forecast_cov()

        @pl.when(n == STEP_PAIR)
        def _():
            send_pair()

        @pl.when(n == STEP_Y)
        def _():
            send_entries()

        @pl.when(n == STEP_CORE)
        def _():
            send_core()
            solve()

        @pl.when(n == STEP_CORR)
        def _():
            correct()

        @pl.when(jnp.logical_and(n >= 2, lax.rem(n, 2) == 0))
        def _():
            advance(lax.div(n, 2) - 1)

        @pl.when(jnp.logical_and(n > STEP_CORR, n < steps - 1))
        def _():
            finish(2 * (n - STEP_CORR - 1))
            finish(2 * (n - STEP_CORR - 1) + 1)

        @pl.when(n >= steps - 1)
        def _():
            finish(n - groups - 1)

        return carry

    lax.fori_loop(0, steps + 1, step, 0)

    for copy in [head_up, head_down, pair_copy(mine), pair_entries(mine), core_copy(core)]:
        copy.wait_send()
    for copy in z_copies:
        copy.wait_send()
    for p in x_peers:
        x_copy(x, p).wait_send()
    for p in y_peers:
        y_copy(y, p).wait_send()
    for target in others:
        entries_copy((core, y), target).wait_send()


def local(
    slab_cols, observed_cov, observed_cells, noise_variance, wind_across, wind_along, diffusion
):
    columns, local_cells = slab_cols.shape
    grid_rows, width = wind_across.shape
    count = observed_cells.shape[1]
    total = 2 * count
    extent = grid_rows + 2 * SECTIONS
    edge = SECTIONS * width
    groups = columns // GROUP
    f32 = jnp.float32
    dma = pltpu.SemaphoreType.DMA
    any_space = pl.BlockSpec(memory_space=pltpu.HBM)
    scalars = pl.BlockSpec(memory_space=pltpu.SMEM)
    operands = [
        pltpu.with_memory_space_constraint(a, pltpu.HBM)
        for a in (
            observed_cells, noise_variance, slab_cols, observed_cov, wind_across, wind_along, diffusion
        )
    ]
    return pl.pallas_call(
        kernel,
        out_shape=pltpu.VMEM((columns, local_cells), f32),
        in_specs=[scalars, scalars] + [any_space] * 5,
        out_specs=pl.BlockSpec(memory_space=pltpu.VMEM),
        scratch_shapes=[
            pltpu.VMEM((columns, local_cells), f32),
            pltpu.VMEM((columns, edge), f32),
            pltpu.VMEM((columns, edge), f32),
            pltpu.VMEM((2, 1, local_cells), f32),
            pltpu.VMEM((5, extent, width), f32),
            pltpu.VMEM((5, extent, width), f32),
            pltpu.VMEM((5, extent, GROUP, width), f32),
            pltpu.VMEM((extent, GROUP, width), f32),
            pltpu.VMEM((extent, GROUP, width), f32),
            pltpu.VMEM((width // LANES, total * grid_rows, LANES), f32),
            pltpu.VMEM((grid_rows, columns, width), f32),
            pltpu.VMEM((columns, LANES), f32),
            pltpu.VMEM((total, LANES), f32),
            pltpu.VMEM((total + GROUP, LANES), f32),
            pltpu.VMEM((4, total + GROUP, LANES), f32),
            pltpu.VMEM((total + GROUP, LANES), f32),
            pltpu.VMEM((4, total + GROUP, LANES), f32),
            pltpu.VMEM((GROUP, LANES), f32),
            pltpu.VMEM((16, GROUP, LANES), f32),
            dma((5,)),
            dma((2, 2 * groups)),
            dma((2, 2 * groups)),
            dma((2,)),
            dma((2,)),
            dma((4,)),
            dma((4,)),
            dma((4,)),
            dma((4,)),
            dma((8,)),
            dma((8,)),
            dma((2,)),
            dma((2,)),
            dma((4,)),
            dma((4,)),
            dma,
            dma,
        ],
        compiler_params=pltpu.CompilerParams(
            collective_id=0, has_side_effects=True, vmem_limit_bytes=32 * 1024 * 1024
        ),
    )(*operands)


def solution(mesh):
    return jax.shard_map(
        local,
        mesh=mesh,
        in_specs=(
            P("cols", "cells"),
            P(None, "cols", "cells"),
            P(),
            P(),
            P("cells", None),
            P("cells", None),
            P("cells", None),
        ),
        out_specs=P("cols", "cells"),
        check_vma=False,
    )
```

time: 78.7 us -> 70 us (0.89)
  Pallas kernels: 75.5 us -> 68.6 us
  local copies, waits for them, and re-layouts: 3.06 us -> 1.32 us
    pallas_call x1, Pallas kernels: 75.5 us -> 68.6 us  [local(): pl.pallas_call(kernel, out_shape=pltpu.VMEM((columns, local_cells), f32),...]
    unnamed x1, local copies, waits for them, and re-layouts: 3.06 us -> 1.32 us
where the time goes in v1:
time: 70 us; the launch traced here: 69.9 us
  Pallas kernels  68.6 us (98%)
  local copies, waits for them, and re-layouts  1.32 us (2%)
    pallas_call x1, Pallas kernels, local(): pl.pallas_call(kernel, out_shape=pltpu.VMEM((columns, local_cells), f32),...  68.6 us

profile of v1, /device:TPU:1, one launch (start us, length us, event | category | flops | bytes accessed | tf_op | source)
XLA Modules:
  0.0 69.9 jit_solution(7880918631660573281)
XLA Ops:
  0.0 68.6 %shard_map.73 = f32[64,8192]{1,0:T(8,128)S(1)} custom-call(s32[2,16]{1,0:T(2,128)} %cells_ref.1, f32[2,16]{1,0:T(2,128)} %noise_ref.1, f32[64,8192]{1,0:T(8,128)} %slab_ref.1, f32[2,1,8192]{2,1,0:T(1,128)} %cov_ref.1, f32[16,512]{1,0:T(8,128)} %across_ref.1, f32[16,512]{1,0:T(8,128)} %along_ref.1, f32[16,512]{1,0:T(8,128)} %spread_ref.1), custom_call_target="tpu_custom_call" | custom-call | tf_op jit(solution)/shard_map/pallas_call | solution.py:466
  68.6 1.3 %copy.9 = f32[64,8192]{1,0:T(8,128)} copy(f32[64,8192]{1,0:T(8,128)S(1)} %shard_map.73) | data formatting | bytes 4194304

commit v2 on v1

--- a/solution.py
+++ b/solution.py
@@ -8,8 +8,9 @@
 SECTIONS = 8
 GROUP = 8
 LANES = 128
+FIRST = 2
 AHEAD = 6
-STEP_X, STEP_PAIR, STEP_Y, STEP_CORE, STEP_CORR = 0, 3, 6, 9, 11
+STEP_HEAD, STEP_PAIR, STEP_Y, STEP_CORE, STEP_CORR = 0, 3, 6, 9, 12
 MESH = pl.DeviceIdType.MESH
 
 
@@ -21,7 +22,7 @@
     cells_ref, noise_ref, slab_ref, cov_ref, across_ref, along_ref, spread_ref, result,
     own, low, high, flat, head, natural, coef, buf_a, buf_b, gathered, corr, weight, right_side,
     msg_x, slots_x, msg_z, slots_z, msg_c, slots_c,
-    local_sem, halo_send, halo_recv, head_send, head_recv,
+    local_sem, halo_send, halo_recv, head_send, head_recv, wind_send, wind_recv, w_send, w_recv,
     x_send, x_recv, z_send, z_recv, e_send, e_recv,
     pair_send, pair_recv, y_send, y_recv, core_send, core_recv,
 ):
@@ -119,36 +120,15 @@
     )
     found = found[0:height] + found[height : 2 * height] + found[2 * height : 3 * height]
     found = jnp.concatenate([found, jnp.zeros((height, LANES - total), jnp.float32)], axis=1)
-    square = jnp.concatenate(
-        [
-            jnp.zeros((total, LANES), jnp.float32),
-            found[0:columns],
-            jnp.zeros((LANES - total - columns, LANES), jnp.float32),
-        ],
-        axis=0,
-    )
-    tile = found[columns : columns + GROUP]
-    msg_z[0:total, :] = square.T[0:total, :]
-    msg_z[total : total + GROUP, :] = tile
-
+    rows = columns // 4
+    packed = found[0:rows]
+    for n in range(1, 4):
+        packed = packed + pltpu.roll(found[n * rows : (n + 1) * rows], n * total, 1)
+    msg_z[0:rows, :] = packed
+    msg_z[rows : rows + GROUP, :] = found[columns : columns + GROUP]
     pl.semaphore_wait(barrier, len(peers))
 
     top = SECTIONS + grid_rows
-    head_up = remote(
-        head.at[:, grid_rows : grid_rows + SECTIONS, :], head.at[:, 0:SECTIONS, :],
-        head_send.at[0], head_recv.at[0], cells_device(after),
-    )
-    head_down = remote(
-        head.at[:, SECTIONS : 2 * SECTIONS, :], head.at[:, top : top + SECTIONS, :],
-        head_send.at[1], head_recv.at[1], cells_device(before),
-    )
-    z_copies = [
-        remote(msg_z, slots_z.at[z_hi], z_send.at[p], z_recv.at[z_hi], cells_device(x * 4 + p)) for p in z_peers
-    ]
-    for copy in z_copies:
-        copy.start()
-    head_up.start()
-    head_down.start()
 
     def halos(n):
         rows = pl.ds(pl.multiple_of(lax.div(n, 2) * GROUP, GROUP), GROUP)
@@ -167,7 +147,47 @@
             ),
         )
 
-    for n in range(AHEAD):
+    quarter = pl.ds(pl.multiple_of(y * LANES, LANES), LANES)
+    wind_rows = pl.ds(pl.multiple_of((1 - core) * (grid_rows - SECTIONS), SECTIONS), SECTIONS)
+    side = lax.select(core == 0, after, before)
+    winds = [
+        remote(
+            ref.at[wind_rows, quarter], head.at[n, pl.ds(pl.multiple_of(core * top, SECTIONS), SECTIONS), quarter],
+            wind_send.at[n], wind_recv.at[n], cells_device(side),
+        )
+        for n, ref in enumerate((across_ref, along_ref, spread_ref))
+    ]
+    others = [(core, p) for p in y_peers] + [(1 - core, p) for p in y_peers] + [(1 - core, y)]
+
+    def wind_copy(source, target):
+        piece = head.at[
+            0:3,
+            pl.ds(pl.multiple_of(source[0] * top, SECTIONS), SECTIONS),
+            pl.ds(pl.multiple_of(source[1] * LANES, LANES), LANES),
+        ]
+        return remote(
+            piece, piece, w_send.at[target[0] * 4 + target[1]], w_recv.at[source[0] * 4 + source[1]],
+            cols_device(z_lo * 8 + target[1] * 2 + target[0]),
+        )
+
+    z_copies = [
+        remote(msg_z, slots_z.at[z_hi], z_send.at[p], z_recv.at[z_hi], cells_device(x * 4 + p)) for p in z_peers
+    ]
+    for copy in z_copies:
+        copy.start()
+    head_up = remote(
+        head.at[3:5, grid_rows : grid_rows + SECTIONS, :], head.at[3:5, 0:SECTIONS, :],
+        head_send.at[0], head_recv.at[0], cells_device(after),
+    )
+    head_down = remote(
+        head.at[3:5, SECTIONS : 2 * SECTIONS, :], head.at[3:5, top : top + SECTIONS, :],
+        head_send.at[1], head_recv.at[1], cells_device(before),
+    )
+    for copy in winds:
+        copy.start()
+    head_up.start()
+    head_down.start()
+    for n in range(FIRST):
         for copy in halos(n):
             copy.start()
 
@@ -199,8 +219,6 @@
     def core_copy(source):
         half = block_of(source * 8, 8)
         return remote(half, half, core_send, core_recv, cols_device(z_lo * 8 + y * 2 + (1 - core)))
-
-    others = [(core, p) for p in y_peers] + [(1 - core, p) for p in y_peers] + [(1 - core, y)]
 
     def entries_copy(source, target):
         mate = source[0] * 4 + source[1]
@@ -257,6 +275,8 @@
             x_copy(x, p).start()
 
     def forecast_cov():
+        for source in others:
+            wind_copy(source, source).wait_recv()
         head_up.wait_recv()
         head_down.wait_recv()
         half_across = 0.5 * head[0]
@@ -300,9 +320,20 @@
         summed = msg_x[...]
         for p in x_peers:
             summed = summed + slots_x[p]
-        right_side[...] = summed[0:total, :]
-        msg_c[...] = summed[total : total + GROUP, :]
-        slots_c[mine] = summed[total : total + GROUP, :]
+        quarter_rows = columns // 4
+        picks = summed[0:quarter_rows]
+        entries = summed[quarter_rows : quarter_rows + GROUP]
+        lane = lax.broadcasted_iota(jnp.int32, (quarter_rows, LANES), 1)
+        picks = [picks] + [pltpu.roll(picks, LANES - n * total, 1) for n in range(1, 4)]
+        square = jnp.concatenate(
+            [jnp.zeros((total, LANES), jnp.float32)]
+            + [jnp.where(lane < total, block, 0.0) for block in picks]
+            + [jnp.zeros((LANES - total - columns, LANES), jnp.float32)],
+            axis=0,
+        )
+        right_side[...] = square.T[0:total, :]
+        msg_c[...] = entries
+        slots_c[mine] = entries
         pair_entries(mine).start()
         pair_copy(other).wait_recv()
         for p in y_peers:
@@ -392,9 +423,8 @@
             for copy in halos(n + AHEAD):
                 copy.start()
 
-        @pl.when(n == STEP_X)
-        def _():
-            send_x()
+        @pl.when(n == STEP_HEAD)
+        def _():
             forecast_cov()
 
         @pl.when(n == STEP_PAIR)
@@ -418,22 +448,27 @@
         def _():
             advance(lax.div(n, 2) - 1)
 
-        @pl.when(jnp.logical_and(n > STEP_CORR, n < steps - 1))
+        @pl.when(n > STEP_CORR)
         def _():
             finish(2 * (n - STEP_CORR - 1))
             finish(2 * (n - STEP_CORR - 1) + 1)
 
-        @pl.when(n >= steps - 1)
-        def _():
-            finish(n - groups - 1)
-
         return carry
+
+    for copy in winds:
+        copy.wait_recv()
+    for target in others:
+        wind_copy((core, y), target).start()
+    send_x()
+    for n in range(FIRST, AHEAD):
+        for copy in halos(n):
+            copy.start()
 
     lax.fori_loop(0, steps + 1, step, 0)
 
     for copy in [head_up, head_down, pair_copy(mine), pair_entries(mine), core_copy(core)]:
         copy.wait_send()
-    for copy in z_copies:
+    for copy in z_copies + winds:
         copy.wait_send()
     for p in x_peers:
         x_copy(x, p).wait_send()
@@ -441,6 +476,7 @@
         y_copy(y, p).wait_send()
     for target in others:
         entries_copy((core, y), target).wait_send()
+        wind_copy((core, y), target).wait_send()
 
 
 def local(
@@ -482,10 +518,10 @@
             pltpu.VMEM((grid_rows, columns, width), f32),
             pltpu.VMEM((columns, LANES), f32),
             pltpu.VMEM((total, LANES), f32),
-            pltpu.VMEM((total + GROUP, LANES), f32),
-            pltpu.VMEM((4, total + GROUP, LANES), f32),
-            pltpu.VMEM((total + GROUP, LANES), f32),
-            pltpu.VMEM((4, total + GROUP, LANES), f32),
+            pltpu.VMEM((columns // 4 + GROUP, LANES), f32),
+            pltpu.VMEM((4, columns // 4 + GROUP, LANES), f32),
+            pltpu.VMEM((columns // 4 + GROUP, LANES), f32),
+            pltpu.VMEM((4, columns // 4 + GROUP, LANES), f32),
             pltpu.VMEM((GROUP, LANES), f32),
             pltpu.VMEM((16, GROUP, LANES), f32),
             dma((5,)),
@@ -493,6 +529,10 @@
             dma((2, 2 * groups)),
             dma((2,)),
             dma((2,)),
+            dma((3,)),
+            dma((3,)),
+            dma((8,)),
+            dma((8,)),
             dma((4,)),
             dma((4,)),
             dma((4,)),

time: 70 us -> 68.3 us (0.976)
  Pallas kernels: 68.6 us -> 66.8 us
    pallas_call x1, Pallas kernels: 68.6 us -> 66.8 us  [local(): pl.pallas_call(kernel, out_shape=pltpu.VMEM((columns, local_cells), f32),...]
where the time goes in v2:
time: 68.3 us; the launch traced here: 68.2 us
  Pallas kernels  66.8 us (98%)
  local copies, waits for them, and re-layouts  1.32 us (2%)
    pallas_call x1, Pallas kernels, local(): pl.pallas_call(kernel, out_shape=pltpu.VMEM((columns, local_cells), f32),...  66.8 us

profile of v2, /device:TPU:1, one launch (start us, length us, event | category | flops | bytes accessed | tf_op | source)
XLA Modules:
  0.0 68.2 jit_solution(10869088002864278181)
XLA Ops:
  0.0 66.8 %shard_map.73 = f32[64,8192]{1,0:T(8,128)S(1)} custom-call(s32[2,16]{1,0:T(2,128)} %cells_ref.1, f32[2,16]{1,0:T(2,128)} %noise_ref.1, f32[64,8192]{1,0:T(8,128)} %slab_ref.1, f32[2,1,8192]{2,1,0:T(1,128)} %cov_ref.1, f32[16,512]{1,0:T(8,128)} %across_ref.1, f32[16,512]{1,0:T(8,128)} %along_ref.1, f32[16,512]{1,0:T(8,128)} %spread_ref.1), custom_call_target="tpu_custom_call" | custom-call | tf_op jit(solution)/shard_map/pallas_call | solution.py:502
  66.9 1.3 %copy.9 = f32[64,8192]{1,0:T(8,128)} copy(f32[64,8192]{1,0:T(8,128)S(1)} %shard_map.73) | data formatting | bytes 4194304

commit v3 on v2

--- a/solution.py
+++ b/solution.py
@@ -9,8 +9,8 @@
 GROUP = 8
 LANES = 128
 FIRST = 2
-AHEAD = 6
-STEP_HEAD, STEP_PAIR, STEP_Y, STEP_CORE, STEP_CORR = 0, 3, 6, 9, 12
+AHEAD = 3
+STEP_HEAD, STEP_PAIR, STEP_Y, STEP_CORE, STEP_CORR = 0, 2, 5, 8, 12
 MESH = pl.DeviceIdType.MESH
 
 
@@ -133,16 +133,17 @@
     def halos(n):
         rows = pl.ds(pl.multiple_of(lax.div(n, 2) * GROUP, GROUP), GROUP)
         piece = edge // 2
-        shift = lax.rem(n, 2) * piece
-        here = pl.ds(pl.multiple_of(shift, piece), piece)
-        last = pl.ds(pl.multiple_of(local_cells - edge + shift, piece), piece)
+        far = lax.rem(n, 2)
+        above = pl.ds(pl.multiple_of(far * piece, piece), piece)
+        below = pl.ds(pl.multiple_of((1 - far) * piece, piece), piece)
+        last = pl.ds(pl.multiple_of(local_cells - edge + (1 - far) * piece, piece), piece)
         return (
             remote(
-                slab_ref.at[rows, last], low.at[rows, here],
+                slab_ref.at[rows, last], low.at[rows, below],
                 halo_send.at[0, n], halo_recv.at[0, n], cells_device(after),
             ),
             remote(
-                slab_ref.at[rows, here], high.at[rows, here],
+                slab_ref.at[rows, above], high.at[rows, above],
                 halo_send.at[1, n], halo_recv.at[1, n], cells_device(before),
             ),
         )
@@ -228,7 +229,7 @@
             cols_device(z_lo * 8 + target[1] * 2 + target[0]),
         )
 
-    def stencil(g):
+    def stencil(g, ranges):
         rows = pl.ds(pl.multiple_of(g * GROUP, GROUP), GROUP)
 
         def read(r, section):
@@ -241,22 +242,22 @@
             return (buf_a if section % 2 else buf_b)[r]
 
         for section in range(SECTIONS):
-            first, last = section + 1, extent - section - 1
-            below, here = read(first - 1, section), read(first, section)
-            for r in range(first, last):
-                above = read(r + 1, section)
-                new = (
-                    coef[0, r] * here
-                    + coef[1, r] * above
-                    + coef[2, r] * below
-                    + coef[3, r] * pltpu.roll(here, width - 1, 1)
-                    + coef[4, r] * pltpu.roll(here, 1, 1)
-                )
-                if section == SECTIONS - 1:
-                    result[rows, (r - SECTIONS) * width : (r - SECTIONS + 1) * width] = new
-                else:
-                    (buf_b if section % 2 else buf_a)[r] = new
-                below, here = here, above
+            for first, last in ranges(section):
+                below, here = read(first - 1, section), read(first, section)
+                for r in range(first, last):
+                    above = read(r + 1, section)
+                    new = (
+                        coef[0, r] * here
+                        + coef[1, r] * above
+                        + coef[2, r] * below
+                        + coef[3, r] * pltpu.roll(here, width - 1, 1)
+                        + coef[4, r] * pltpu.roll(here, 1, 1)
+                    )
+                    if section == SECTIONS - 1:
+                        result[rows, (r - SECTIONS) * width : (r - SECTIONS + 1) * width] = new
+                    else:
+                        (buf_b if section % 2 else buf_a)[r] = new
+                    below, here = here, above
 
     def finish(g):
         rows = pl.ds(pl.multiple_of(g * GROUP, GROUP), GROUP)
@@ -404,15 +405,25 @@
 
         lax.fori_loop(0, grid_rows, one_row, 0)
 
-    def advance(g):
-        for h in range(2):
-            for copy in halos(2 * g + h):
-                copy.wait_recv()
-        stencil(g)
+    near = SECTIONS // 2
+
+    def begin(g):
+        for copy in halos(2 * g):
+            copy.wait_recv()
+        stencil(g, lambda s: [(near + s + 1, extent - near - s - 1)])
+
+    def end(g):
+        for copy in halos(2 * g + 1):
+            copy.wait_recv()
+        stencil(g, lambda s: [(s + 1, near + s + 1), (extent - near - s - 1, extent - s - 1)])
 
     steps = 2 * groups
 
     def step(n, carry):
+        @pl.when(lax.rem(n, 2) == 1)
+        def _():
+            begin(lax.div(n, 2))
+
         @pl.when(n < steps)
         def _():
             for copy in halos(n):
@@ -446,7 +457,7 @@
 
         @pl.when(jnp.logical_and(n >= 2, lax.rem(n, 2) == 0))
         def _():
-            advance(lax.div(n, 2) - 1)
+            end(lax.div(n, 2) - 1)
 
         @pl.when(n > STEP_CORR)
         def _():

time: 68.3 us -> 67.8 us (level)
  the two profiles are of different devices: /device:TPU:1 before, /device:TPU:8 now
where the time goes in v3:
time: 67.8 us; the launch traced here: 67.7 us
  Pallas kernels  66.4 us (98%)
  local copies, waits for them, and re-layouts  1.32 us (2%)
    pallas_call x1, Pallas kernels, local(): pl.pallas_call(kernel, out_shape=pltpu.VMEM((columns, local_cells), f32),...  66.4 us

profile of v3, /device:TPU:8, one launch (start us, length us, event | category | flops | bytes accessed | tf_op | source)
XLA Modules:
  0.0 67.7 jit_solution(15778567189530183088)
XLA Ops:
  0.0 66.4 %shard_map.73 = f32[64,8192]{1,0:T(8,128)S(1)} custom-call(s32[2,16]{1,0:T(2,128)} %cells_ref.1, f32[2,16]{1,0:T(2,128)} %noise_ref.1, f32[64,8192]{1,0:T(8,128)} %slab_ref.1, f32[2,1,8192]{2,1,0:T(1,128)} %cov_ref.1, f32[16,512]{1,0:T(8,128)} %across_ref.1, f32[16,512]{1,0:T(8,128)} %along_ref.1, f32[16,512]{1,0:T(8,128)} %spread_ref.1), custom_call_target="tpu_custom_call" | custom-call | tf_op jit(solution)/shard_map/pallas_call | solution.py:513
  66.4 1.3 %copy.9 = f32[64,8192]{1,0:T(8,128)} copy(f32[64,8192]{1,0:T(8,128)S(1)} %shard_map.73) | data formatting | bytes 4194304

commit v4 on v3

--- a/solution.py
+++ b/solution.py
@@ -10,7 +10,7 @@
 LANES = 128
 FIRST = 2
 AHEAD = 3
-STEP_HEAD, STEP_PAIR, STEP_Y, STEP_CORE, STEP_CORR = 0, 2, 5, 8, 12
+STEP_HEAD, STEP_PAIR, STEP_Y, STEP_CORE, STEP_CORR, STEP_END = 0, 2, 5, 8, 10, 12
 MESH = pl.DeviceIdType.MESH
 
 
@@ -459,10 +459,10 @@
         def _():
             end(lax.div(n, 2) - 1)
 
-        @pl.when(n > STEP_CORR)
-        def _():
-            finish(2 * (n - STEP_CORR - 1))
-            finish(2 * (n - STEP_CORR - 1) + 1)
+        @pl.when(n > STEP_END)
+        def _():
+            finish(2 * (n - STEP_END - 1))
+            finish(2 * (n - STEP_END - 1) + 1)
 
         return carry
 

time: 67.8 us -> 67.8 us (level)
  no operation moved by 1% of the time
where the time goes in v4:
time: 67.8 us; the launch traced here: 67.7 us
  Pallas kernels  66.4 us (98%)
  local copies, waits for them, and re-layouts  1.32 us (2%)
    pallas_call x1, Pallas kernels, local(): pl.pallas_call(kernel, out_shape=pltpu.VMEM((columns, local_cells), f32),...  66.4 us

profile of v4, /device:TPU:8, one launch (start us, length us, event | category | flops | bytes accessed | tf_op | source)
XLA Modules:
  0.0 67.7 jit_solution(3981746709137061383)
XLA Ops:
  0.0 66.4 %shard_map.73 = f32[64,8192]{1,0:T(8,128)S(1)} custom-call(s32[2,16]{1,0:T(2,128)} %cells_ref.1, f32[2,16]{1,0:T(2,128)} %noise_ref.1, f32[64,8192]{1,0:T(8,128)} %slab_ref.1, f32[2,1,8192]{2,1,0:T(1,128)} %cov_ref.1, f32[16,512]{1,0:T(8,128)} %across_ref.1, f32[16,512]{1,0:T(8,128)} %along_ref.1, f32[16,512]{1,0:T(8,128)} %spread_ref.1), custom_call_target="tpu_custom_call" | custom-call | tf_op jit(solution)/shard_map/pallas_call | solution.py:513
  66.4 1.3 %copy.9 = f32[64,8192]{1,0:T(8,128)} copy(f32[64,8192]{1,0:T(8,128)S(1)} %shard_map.73) | data formatting | bytes 4194304

commit v5 on v4

--- a/solution.py
+++ b/solution.py
@@ -8,7 +8,7 @@
 SECTIONS = 8
 GROUP = 8
 LANES = 128
-FIRST = 2
+FIRST = 3
 AHEAD = 3
 STEP_HEAD, STEP_PAIR, STEP_Y, STEP_CORE, STEP_CORR, STEP_END = 0, 2, 5, 8, 10, 12
 MESH = pl.DeviceIdType.MESH

time: 67.8 us -> 67.8 us (level)
  the two profiles are of different devices: /device:TPU:8 before, /device:TPU:1 now
where the time goes in v5:
time: 67.8 us; the launch traced here: 67.4 us
  Pallas kernels  66.1 us (97%)
  local copies, waits for them, and re-layouts  1.32 us (2%)
    pallas_call x1, Pallas kernels, local(): pl.pallas_call(kernel, out_shape=pltpu.VMEM((columns, local_cells), f32),...  66.1 us

profile of v5, /device:TPU:1, one launch (start us, length us, event | category | flops | bytes accessed | tf_op | source)
XLA Modules:
  0.0 67.4 jit_solution(15019270950264382707)
XLA Ops:
  0.0 66.1 %shard_map.73 = f32[64,8192]{1,0:T(8,128)S(1)} custom-call(s32[2,16]{1,0:T(2,128)} %cells_ref.1, f32[2,16]{1,0:T(2,128)} %noise_ref.1, f32[64,8192]{1,0:T(8,128)} %slab_ref.1, f32[2,1,8192]{2,1,0:T(1,128)} %cov_ref.1, f32[16,512]{1,0:T(8,128)} %across_ref.1, f32[16,512]{1,0:T(8,128)} %along_ref.1, f32[16,512]{1,0:T(8,128)} %spread_ref.1), custom_call_target="tpu_custom_call" | custom-call | tf_op jit(solution)/shard_map/pallas_call | solution.py:513
  66.1 1.3 %copy.9 = f32[64,8192]{1,0:T(8,128)} copy(f32[64,8192]{1,0:T(8,128)S(1)} %shard_map.73) | data formatting | bytes 4194304
